TPU v7x, 256 devices: a whole 4x4x8 slice. The times are simulated.
256 devices in a mesh: dp: 8 (over y_hi, x), shard: 32 (over z, y_lo, core).
Axes of the slice: x: 4, y: 4 (y_hi: 2, y_lo: 2; y = y_hi * 2 + y_lo), z: 8, core: 2. Of those that a mesh axis runs over, the one named last changes fastest.
Arguments:
- tokens: bfloat16 [65536, 8192], P(('dp', 'shard')), may hold values from -6 to 6
- out_grad: bfloat16 [65536, 8192], P(('dp', 'shard')), may hold values from -0.0234375 to 0.0234375
- projector: bfloat16 [8192, 512], P(('dp', 'shard')), may hold values from -0.0625 to 0.0625
- first_moment: float32 [512, 8192], P('dp', 'shard'), may hold values from -6 to 6
- second_moment: float32 [512, 8192], P('dp', 'shard'), may hold values from 0.25 to 4
Outputs:
- first_new: float32 [512, 8192], P('dp', 'shard')
- second_new: float32 [512, 8192], P('dp', 'shard')
- update: bfloat16 [8192, 8192], P('dp', 'shard')
All inputs are finite; a program needn't handle non-finite values.
Results may differ from a plain program's by a relative error of at most 0.0038.
The roundings to bfloat16 on the way count: a program that leaves them out, or rounds other values in their place, can miss the bound.
Values may be sent and summed in bfloat16 or wider, within the bound.
A program may use at most 128 MiB of HBM per device.

v0:
```python
import jax
import jax.numpy as jnp
from jax import lax
from jax.sharding import PartitionSpec as P

beta_one = 0.9
beta_two = 0.999
adam_epsilon = 1e-08


def on_device(tokens, out_grad, projector, first_moment, second_moment):
    group_rows = projector.shape[0] * lax.axis_size("shard")
    whole = lax.all_gather(projector, ("dp", "shard"), axis=0, tiled=True)
    projected = jnp.dot(tokens, whole, preferred_element_type=jnp.float32)
    local_rows = lax.dynamic_slice_in_dim(whole, lax.axis_index("dp") * group_rows, group_rows, 0)
    projected = projected.astype(jnp.bfloat16)
    partial_value = lax.dot_general(
        projected, out_grad, (((0,), (0,)), ((), ())), preferred_element_type=jnp.float32
    )
    column_sum = lax.psum_scatter(partial_value, "shard", scatter_dimension=1, tiled=True)
    low_grad = lax.psum_scatter(column_sum, "dp", scatter_dimension=0, tiled=True)
    first_new = beta_one * first_moment + (1.0 - beta_one) * low_grad
    second_new = beta_two * second_moment + (1.0 - beta_two) * low_grad * low_grad
    direction = (first_new / (jnp.sqrt(second_new) + adam_epsilon)).astype(jnp.bfloat16)
    update = jnp.dot(
        local_rows,
        lax.all_gather(direction, "dp", axis=0, tiled=True),
        preferred_element_type=jnp.float32,
    )
    return (first_new, second_new, update.astype(jnp.bfloat16))


def solution(mesh):
    in_specs = (
        P(("dp", "shard"), None),
        P(("dp", "shard"), None),
        P(("dp", "shard"), None),
        P("dp", "shard"),
        P("dp", "shard"),
    )
    out_specs = (P("dp", "shard"), P("dp", "shard"), P("dp", "shard"))
    return jax.shard_map(
        on_device, mesh=mesh, in_specs=in_specs, out_specs=out_specs, check_vma=False
    )
```

profile of v0, /device:TPU:32, one launch (start us, length us, event | category | flops | bytes accessed | tf_op | source)
XLA Modules:
  0.0 760.5 jit_solution(3993529770521192579)
XLA Ops:
  7.2 0.0 all-gather.2.cloned.1.call-start
  7.2 0.7 all-gather.2.cloned.1.call-update
  7.9 0.0 reduce-scatter.3.cloned.1.call-start
  7.9 424.8 %all-gather.2.cloned.1.call-done = bf16[8192,512]{1,0:T(8,128)(2,1)} async-done(((bf16[32,512]{1,0:T(8,128)(2,1)}), bf16[8192,512]{1,0:T(8,128)(2,1)}) %all-gather.2.cloned.1.call-update) | async-done | bytes 8388624 | tf_op jit(solution)/shard_map/all_gather | solution.py:13
  432.7 16.2 %fusion.1 = f32[512,8192]{1,0:T(8,128)} fusion(bf16[256,8192]{1,0:T(8,128)(2,1)} %param.6, bf16[256,8192]{1,0:T(8,128)(2,1)} %param.5, bf16[8192,512]{1,0:T(8,128)(2,1)} %all-gather.2.cloned.1.call-done), kind=kOutput, calls=%fused_computation.3 | convolution fusion | flops 4295098368 | bytes 33554432 | tf_op jit(solution)/shard_map/dot_general | solution.py:17
  448.9 0.0 copy-start
  448.9 0.0 copy-start.1
  448.9 0.0 reduce-scatter.3.cloned.1.call-update
  448.9 0.0 reduce-scatter.5.cloned.1.call-start
  449.0 183.0 %reduce-scatter.3.cloned.1.call-done = f32[512,256]{1,0:T(8,128)} async-done(((f32[512,8192]{1,0:T(8,128)}), f32[512,256]{1,0:T(8,128)}) %reduce-scatter.3.cloned.1.call-update) | async-done | bytes 524304 | tf_op jit(solution)/shard_map/reduce_scatter | solution.py:20
  631.9 0.0 reduce-scatter.5.cloned.1.call-update
  632.0 83.7 %reduce-scatter.5.cloned.1.call-done = f32[64,256]{1,0:T(8,128)} async-done(((f32[512,256]{1,0:T(8,128)}), f32[64,256]{1,0:T(8,128)}) %reduce-scatter.5.cloned.1.call-update) | async-done | bytes 65552 | tf_op jit(solution)/shard_map/reduce_scatter | solution.py:21
  715.6 0.0 copy-done
  715.6 0.0 copy-done.1
  715.6 1.5 divide_convert_fusion
  717.1 34.4 %all_gather.7 = bf16[512,256]{1,0:T(8,128)(2,1)S(1)} all-gather(bf16[64,256]{1,0:T(8,128)(2,1)S(1)} %get-tuple-element.3), channel_id=1, replica_groups=mesh['dp'=8,'shard'=32] {'dp'}, dimensions={0}, use_global_device_ids=true | all-gather | bytes 294912 | tf_op jit(solution)/shard_map/all_gather | solution.py:27
  751.5 2.5 convolution_convert_fusion
Async XLA Ops:
  7.2 425.5 %all-gather.2.cloned.1.call-start = ((), (), s32[]{:S(2)}) async-start(), calls=%async_computation.2 | async-start | bytes 8421376 | tf_op jit(solution)/shard_map/all_gather | solution.py:13
  7.9 624.0 %reduce-scatter.3.cloned.1.call-start = ((), (), s32[]{:S(2)}) async-start(), calls=%async_computation.3 | async-start | bytes 17301504 | tf_op jit(solution)/shard_map/reduce_scatter | solution.py:20
  448.9 266.7 %copy-start = (f32[64,256]{1,0:T(8,128)S(1)}, f32[64,256]{1,0:T(8,128)}, u32[]{:S(2)}) copy-start(f32[64,256]{1,0:T(8,128)} %param.9) | copy-start | bytes 196612
  448.9 266.7 %copy-start.1 = (f32[64,256]{1,0:T(8,128)S(1)}, f32[64,256]{1,0:T(8,128)}, u32[]{:S(2)}) copy-start(f32[64,256]{1,0:T(8,128)} %param.8) | copy-start | bytes 196612
  448.9 266.7 %reduce-scatter.5.cloned.1.call-start = ((), (), s32[]{:S(2)}) async-start(), calls=%async_computation.4 | async-start | bytes 589824 | tf_op jit(solution)/shard_map/reduce_scatter | solution.py:21
Sparse Core Ops, SparseCore 0:
  9.9 422.7 all-gather.1
  449.0 182.8 reduce-scatter.2
  635.8 79.7 reduce-scatter.4
where the time goes:
time: 761 us
  waiting for transfers between devices  692 us (91%)
  blocking collectives  34.4 us (5%)
  matrix products  18.6 us (2%)
  between operations  13.8 us (2%)
    all_gather x1, waiting for transfers between devices, on_device(): whole = lax.all_gather(projector, ('dp', 'shard'), axis=0, tiled=True)  425 us
    reduce_scatter x1, waiting for transfers between devices, on_device(): lax.psum_scatter(partial_value, 'shard', scatter_dimension=1, tiled=True)  183 us
    reduce_scatter x1, waiting for transfers between devices, on_device(): lax.psum_scatter(column_sum, 'dp', scatter_dimension=0, tiled=True)  83.7 us
    all_gather x1, blocking collectives, on_device(): lax.all_gather(direction, 'dp', axis=0, tiled=True)  34.4 us
    dot_general x1, matrix products, on_device(): lax.dot_general(projected, out_grad, (((0,), (0,)), ((), ())), preferred_...  16.2 us
  transfers between devices with their start and end apart: 3, of which 3 were waited for; matrix products, arithmetic and copies ran while one was open for 0% of the time, Pallas kernels for 0%

commit v1 on v0

v1 whole, which is shorter than its diff:
```python
import jax
import jax.numpy as jnp
from jax import lax
from jax.experimental import pallas as pl
from jax.experimental.pallas import tpu as pltpu
from jax.sharding import PartitionSpec as P

MESH = pl.DeviceIdType.MESH
beta_one = 0.9
beta_two = 0.999
adam_epsilon = 1e-08
NX, NY, NZ = 4, 4, 8
NCH = 4
ZC = NZ // NCH
CW = ZC * 128
BF = jnp.bfloat16
F32 = jnp.float32


def kernel(tok_ref, grad_ref, proj_ref, m1_ref, m2_ref, o1_ref, o2_ref, up_ref,
           T, OG, S, W, LR, ACC, PJT, PT, RB1, RC1, SB, SC, RB2, RC2, T3, R3, D,
           loc_sem, ex_s, ex_r, zs, zr, ms, mr, fs, fr, lr_sem, pj_sem,
           s1, r1, s2, r2, s3, r3, ds, dr):
    dp = lax.axis_index("dp")
    sh = lax.axis_index("shard")
    x, yh = lax.rem(dp, NX), dp // NX
    z, yl, c = sh // 4, lax.rem(sh // 2, 2), lax.rem(sh, 2)
    y = yh * 2 + yl

    def dev(x_, y_, z_, c_):
        return ((y_ // 2) * NX + x_, z_ * 4 + lax.rem(y_, 2) * 2 + c_)

    def xp(k):
        return lax.rem(x + k, NX)

    def yp(k):
        return lax.rem(y + k, NY)

    def zp(k):
        return lax.rem(z + k, NZ)

    sib = dev(x, y, z, 1 - c)

    def rcopy(src, dst, ss, rs, device):
        return pltpu.make_async_remote_copy(src_ref=src, dst_ref=dst, send_sem=ss, recv_sem=rs,
                                            device_id=device, device_id_type=MESH)

    tok_own = pltpu.make_async_copy(tok_ref, T.at[c], loc_sem.at[0])
    tok_own.start()

    def og_src(par, cls, yl_, z_):
        return grad_ref.at[:, pl.ds(pl.multiple_of(z_ * 1024 + yl_ * 512 + par * 256 + cls * 128, 128), 128)]

    def og_dst(cls, yl_, z_):
        return OG.at[c, cls, yl_, z_ // ZC, :, pl.ds((z_ % ZC) * 128, 128)]

    for cls in range(2):
        for yl_ in range(2):
            for z_ in range(NZ):
                pltpu.make_async_copy(og_src(c, cls, yl_, z_), og_dst(cls, yl_, z_), loc_sem.at[1]).start()
    for h in range(2):
        for cls in range(2):
            S[h, cls] = proj_ref[:, h * 256 + cls * 128:h * 256 + cls * 128 + 128]

    barrier = pltpu.get_barrier_semaphore()
    peers = [sib]
    for k in range(1, NZ):
        peers += [dev(x, y, zp(k), c), dev(x, y, zp(k), 1 - c)]
    for k in range(1, 4):
        peers += [dev(xp(k), y, z, c), dev(x, yp(k), z, c), dev(xp(k), yp(2), z, c)]
    for p in peers:
        pl.semaphore_signal(barrier, inc=1, device_id=p, device_id_type=MESH)
    pl.semaphore_wait(barrier, len(peers))

    W[:, yh, x, z, yl, pl.ds(pl.multiple_of(c * 32, 32), 32), :] = S[c]
    z_copies = []
    for k in range(NZ):
        for rel in range(2):
            if k == 0 and rel == 0:
                continue
            t = c if rel == 0 else 1 - c
            cp = rcopy(S.at[t], W.at[:, yh, x, z, yl, pl.ds(pl.multiple_of(c * 32, 32), 32)],
                       zs.at[k, rel], zr.at[k, rel], dev(x, y, zp(k), t))
            cp.start()
            z_copies.append(cp)

    tok_ex = rcopy(tok_ref, T.at[c], ex_s.at[0], ex_r.at[0], sib)
    tok_ex.start()
    for cls in range(2):
        for yl_ in range(2):
            for z_ in range(NZ):
                rcopy(og_src(1 - c, cls, yl_, z_), og_dst(cls, yl_, z_), ex_s.at[1], ex_r.at[1], sib).start()
    og_ex = rcopy(OG.at[c], OG.at[1 - c], ex_s.at[1], ex_r.at[1], sib)

    for cp in z_copies:
        cp.wait()

    mid = [[None] * 4, [None] * 4]
    fin = []

    def forward(cls, j):
        if cls == 0:
            blk = W.at[0, yh, lax.rem(x + NX - j, NX), :, yl]
        else:
            q = lax.rem(y + NY - j, NY)
            blk = W.at[1, q // 2, x, :, lax.rem(q, 2)]
        for k in range(1, 4):
            to = dev(x, yp(k), z, c) if cls == 0 else dev(xp(k), y, z, c)
            cp = rcopy(blk, blk, fs.at[cls, j, k], fr.at[cls, j, k], to)
            cp.start()
            fin.append(cp)

    for k in range(1, 4):
        for cls in range(2):
            blk = W.at[cls, yh, x, :, yl]
            to = dev(xp(k), y, z, c) if cls == 0 else dev(x, yp(k), z, c)
            mid[cls][k] = rcopy(blk, blk, ms.at[cls, k], mr.at[cls, k], to)
            mid[cls][k].start()
    for cls in range(2):
        forward(cls, 0)
    for j in (1, 3, 2):
        for cls in range(2):
            mid[cls][j].wait_recv()
            forward(cls, j)
    for j in range(1, 4):
        for cls in range(2):
            mid[cls][j].wait_send()
    for cp in fin:
        cp.wait()

    lr_copy = rcopy(W.at[:, yh, x], LR, lr_sem.at[0], lr_sem.at[1], sib)
    lr_copy.start()
    tok_own.wait()
    tok_ex.wait()

    ACC[...] = jnp.zeros_like(ACC)

    def proj_step(k, _):
        w0 = W[0, k // 4, lax.rem(k, 4)].reshape(1024, 128)
        w1 = W[1, k // 4, lax.rem(k, 4)].reshape(1024, 128)
        w = jnp.concatenate([w0, w1], axis=1)
        for t in range(2):
            tk = T[t, :, pl.ds(pl.multiple_of(k * 1024, 1024), 1024)]
            ACC[pl.ds(t * 256, 256), :] += jnp.dot(tk, w, preferred_element_type=F32)
        return 0

    lax.fori_loop(0, 8, proj_step, 0)
    PJT[c] = ACC[...].T.astype(BF)
    pj_copy = rcopy(PJT.at[c], PJT.at[c], pj_sem.at[0], pj_sem.at[1], sib)
    pj_copy.start()
    pltpu.make_async_copy(OG.at[c], OG.at[c], loc_sem.at[1]).wait()
    og_ex.wait()
    pj_copy.wait()

    ph1, ph2 = [], []
    for ch in range(NCH):
        def part_step(i, _, ch=ch):
            cls, yl_ = i // 2, lax.rem(i, 2)
            for r in range(2):
                v = jnp.dot(PJT[r, :, 0:256], OG[0, cls, yl_, ch], preferred_element_type=F32)
                v = v + jnp.dot(PJT[r, :, 256:512], OG[1, cls, yl_, ch], preferred_element_type=F32)
                PT[cls, ch, yl_, r] = v.astype(BF).reshape(4, 64, CW)
            return 0

        lax.fori_loop(0, 4, part_step, 0)
        cps = []
        for k in range(1, 4):
            q = yp(k)
            cps.append(rcopy(PT.at[0, ch, lax.rem(q, 2), q // 2], RB1.at[ch, k - 1],
                             s1.at[0, ch, k], r1.at[0, ch, k], dev(x, q, z, c)))
            cps.append(rcopy(PT.at[1, ch, :, :, xp(k)], RC1.at[ch, k - 1],
                             s1.at[1, ch, k], r1.at[1, ch, k], dev(xp(k), y, z, c)))
        for cp in cps:
            cp.start()
        ph1.append(cps)

    ph3 = []
    for step in range(NCH + 1):
        if step < NCH:
            ch = step
            for cp in ph1[ch]:
                cp.wait_recv()
            vb = PT[0, ch, yl, yh].astype(F32)
            vc = PT[1, ch, :, :, x].astype(F32)
            for k in range(3):
                vb = vb + RB1[ch, k].astype(F32)
                vc = vc + RC1[ch, k].astype(F32)
            SB[ch] = vb
            SC[ch] = vc
            cps = []
            for k in range(1, 4):
                q = yp(k)
                cps.append(rcopy(SB.at[ch, xp(k)], RB2.at[ch, k - 1],
                                 s2.at[0, ch, k], r2.at[0, ch, k], dev(xp(k), y, z, c)))
                cps.append(rcopy(SC.at[ch, lax.rem(q, 2), q // 2], RC2.at[ch, k - 1],
                                 s2.at[1, ch, k], r2.at[1, ch, k], dev(x, q, z, c)))
            for cp in cps:
                cp.start()
            ph2.append(cps)
        if step >= 1:
            ch = step - 1
            for cp in ph2[ch]:
                cp.wait_recv()
            vb = SB[ch, x] + RB2[ch, 0] + RB2[ch, 1] + RB2[ch, 2]
            vc = SC[ch, yl, yh] + RC2[ch, 0] + RC2[ch, 1] + RC2[ch, 2]
            for i in range(ZC):
                T3[ch * ZC + i, 0] = vb[:, i * 128:(i + 1) * 128]
                T3[ch * ZC + i, 1] = vc[:, i * 128:(i + 1) * 128]
                to = ch * ZC + i

                @pl.when(to != z)
                def _(to=to):
                    rcopy(T3.at[to], R3.at[z], s3.at[to], r3.at[z], dev(x, y, to, c)).start()

    R3[z] = T3[z]
    for k in range(1, NZ):
        q = zp(k)
        rcopy(T3.at[q], R3.at[q], s3.at[q], r3.at[q], dev(x, y, q, c)).wait()

    g0 = R3[0]
    for k in range(1, NZ):
        g0 = g0 + R3[k]
    g = jnp.concatenate([g0[0], g0[1]], axis=1)
    first = beta_one * m1_ref[...] + (1.0 - beta_one) * g
    second = beta_two * m2_ref[...] + (1.0 - beta_two) * g * g
    o1_ref[...] = first
    o2_ref[...] = second
    D[dp] = (first / (jnp.sqrt(second) + adam_epsilon)).astype(BF)
    d_copies = []
    for k in range(1, 8):
        q = lax.rem(dp + k, 8)
        cp = rcopy(D.at[dp], D.at[dp], ds.at[k], dr.at[k], (q, sh))
        cp.start()
        d_copies.append(cp)
    for cps in ph1 + ph2:
        for cp in cps:
            cp.wait_send()
    lr_copy.wait()
    for cp in d_copies:
        cp.wait()
    d_own = D[pl.ds(c * 4, 4)].reshape(256, 256)
    d_sib = D[pl.ds((1 - c) * 4, 4)].reshape(256, 256)
    for b in range(4):
        own = jnp.concatenate([W[h, yh, x, 2 * b:2 * b + 2].reshape(256, 128) for h in range(2)], axis=1)
        oth = jnp.concatenate([LR[h, 2 * b:2 * b + 2].reshape(256, 128) for h in range(2)], axis=1)
        u = jnp.dot(own, d_own, preferred_element_type=F32) + jnp.dot(oth, d_sib, preferred_element_type=F32)
        up_ref[b * 256:(b + 1) * 256, :] = u.astype(BF)


def on_device(tokens, out_grad, projector, first_moment, second_moment):
    vm = pl.BlockSpec(memory_space=pltpu.VMEM)
    hbm = pl.BlockSpec(memory_space=pl.ANY)
    dma = pltpu.SemaphoreType.DMA
    return pl.pallas_call(
        kernel,
        out_shape=(
            jax.ShapeDtypeStruct((64, 256), F32),
            jax.ShapeDtypeStruct((64, 256), F32),
            jax.ShapeDtypeStruct((1024, 256), BF),
        ),
        in_specs=[hbm, hbm, vm, vm, vm],
        out_specs=(vm, vm, vm),
        scratch_shapes=[
            pltpu.VMEM((2, 256, 8192), BF),
            pltpu.VMEM((2, 2, 2, NCH, 256, CW), BF),
            pltpu.VMEM((2, 2, 32, 128), BF),
            pltpu.VMEM((2, 2, 4, 8, 2, 64, 128), BF),
            pltpu.VMEM((2, 8, 2, 64, 128), BF),
            pltpu.VMEM((512, 256), F32),
            pltpu.VMEM((2, 256, 512), BF),
            pltpu.VMEM((2, NCH, 2, 2, 4, 64, CW), BF),
            pltpu.VMEM((NCH, 3, 4, 64, CW), BF),
            pltpu.VMEM((NCH, 3, 2, 2, 64, CW), BF),
            pltpu.VMEM((NCH, 4, 64, CW), F32),
            pltpu.VMEM((NCH, 2, 2, 64, CW), F32),
            pltpu.VMEM((NCH, 3, 64, CW), F32),
            pltpu.VMEM((NCH, 3, 64, CW), F32),
            pltpu.VMEM((8, 2, 64, 128), F32),
            pltpu.VMEM((8, 2, 64, 128), F32),
            pltpu.VMEM((8, 64, 256), BF),
            dma((2,)), dma((2,)), dma((2,)),
            dma((8, 2)), dma((8, 2)),
            dma((2, 4)), dma((2, 4)),
            dma((2, 4, 4)), dma((2, 4, 4)),
            dma((2,)), dma((2,)),
            dma((2, NCH, 4)), dma((2, NCH, 4)),
            dma((2, NCH, 4)), dma((2, NCH, 4)),
            dma((8,)), dma((8,)),
            dma((8,)), dma((8,)),
        ],
        compiler_params=pltpu.CompilerParams(
            collective_id=0, has_side_effects=True, vmem_limit_bytes=56 * 2**20
        ),
        name="galore",
    )(tokens, out_grad, projector, first_moment, second_moment)


def solution(mesh):
    in_specs = (
        P(("dp", "shard"), None),
        P(("dp", "shard"), None),
        P(("dp", "shard"), None),
        P("dp", "shard"),
        P("dp", "shard"),
    )
    out_specs = (P("dp", "shard"), P("dp", "shard"), P("dp", "shard"))
    return jax.shard_map(
        on_device, mesh=mesh, in_specs=in_specs, out_specs=out_specs, check_vma=False
    )
```

time: 761 us -> 117 us (0.15)
  the two profiles are of different devices: /device:TPU:32 before, /device:TPU:1 now
where the time goes in v1:
time: 117 us; the launch traced here: 116 us
  Pallas kernels  111 us (95%)
  local copies, waits for them, and re-layouts  4.81 us (4%)
    pallas_call x1, Pallas kernels, on_device(): pl.pallas_call(kernel, out_shape=(jax.ShapeDtypeStruct((64, 256), F32), j...  111 us
    unnamed x3, local copies, waits for them, and re-layouts  4.81 us

profile of v1, /device:TPU:1, one launch (start us, length us, event | category | flops | bytes accessed | tf_op | source)
XLA Modules:
  0.0 116.4 jit_solution(2734914601552141017)
XLA Ops:
  0.6 111.0 %galore.1 = (f32[64,256]{1,0:T(8,128)}, f32[64,256]{1,0:T(8,128)}, bf16[1024,256]{1,0:T(8,128)(2,1)}) custom-call(bf16[256,8192]{1,0:T(8,128)(2,1)} %tok_ref.1, bf16[256,8192]{1,0:T(8,128)(2,1)} %grad_ref.1, bf16[32,512]{1,0:T(8,128)(2,1)} %proj_ref.1, f32[64,256]{1,0:T(8,128)} %m1_ref.1, f32[64,256]{1,0:T(8,128)} %m2_ref.1), custom_call_target="tpu_custom_call" | custom-call | tf_op jit(solution)/shard_map/galore/pallas_call | solution.py:254
  111.6 1.5 %copy.11 = f32[64,256]{1,0:T(8,128)} copy(f32[64,256]{1,0:T(8,128)} %get-tuple-element.6) | data formatting | bytes 131072
  113.1 1.5 %copy.12 = f32[64,256]{1,0:T(8,128)} copy(f32[64,256]{1,0:T(8,128)} %get-tuple-element.7) | data formatting | bytes 131072
  114.6 1.9 %copy.13 = bf16[1024,256]{1,0:T(8,128)(2,1)} copy(bf16[1024,256]{1,0:T(8,128)(2,1)} %get-tuple-element.8) | data formatting | bytes 1048576

commit v2 on v0

v2 whole, which is shorter than its diff:
```python
import jax
import jax.numpy as jnp
from jax import lax
from jax.experimental import pallas as pl
from jax.experimental.pallas import tpu as pltpu
from jax.sharding import PartitionSpec as P

MESH = pl.DeviceIdType.MESH
beta_one = 0.9
beta_two = 0.999
adam_epsilon = 1e-08
NX, NY, NZ = 4, 4, 8
NCH = 4
ZC = NZ // NCH
CW = ZC * 128
BF = jnp.bfloat16
F32 = jnp.float32


def kernel(tok_ref, grad_ref, proj_ref, m1_ref, m2_ref, o1_ref, o2_ref, up_ref,
           T, OG, PJ, M1, M2, S, W, LR, ACC, PJT, PT, PF, RL, AGB, R1, SB, SC, R2, T3, R3, D,
           loc_sem, ex_s, ex_r, zr, mr, fr, lr_sem, pj_sem, r1, rf, r2, snd, rcv):
    dp = lax.axis_index("dp")
    sh = lax.axis_index("shard")
    x, yh = lax.rem(dp, NX), dp // NX
    z, yl, c = sh // 4, lax.rem(sh // 2, 2), lax.rem(sh, 2)
    y = yh * 2 + yl

    def dev(x_, y_, z_, c_):
        return ((y_ // 2) * NX + x_, z_ * 4 + lax.rem(y_, 2) * 2 + c_)

    def xp(k):
        return lax.rem(x + k, NX)

    def yp(k):
        return lax.rem(y + k, NY)

    def zp(k):
        return lax.rem(z + k, NZ)

    sib = dev(x, y, z, 1 - c)

    def arrived(rows, columns, sem):
        ref = T.at[0, 0:rows, 0:columns]
        pltpu.make_async_copy(ref, ref, sem).wait()

    def rcopy(src, dst, ss, rs, device):
        return pltpu.make_async_remote_copy(src_ref=src, dst_ref=dst, send_sem=ss, recv_sem=rs,
                                            device_id=device, device_id_type=MESH)

    barrier = pltpu.get_barrier_semaphore()
    peers = [sib]
    for k in range(1, NZ):
        peers += [dev(x, y, zp(k), c), dev(x, y, zp(k), 1 - c)]
    for k in range(1, 4):
        peers += [dev(xp(k), y, z, c), dev(x, yp(k), z, c), dev(xp(k), yp(2), z, c)]
    for p in peers:
        pl.semaphore_signal(barrier, inc=1, device_id=p, device_id_type=MESH)

    tok_own = pltpu.make_async_copy(tok_ref, T.at[c], loc_sem.at[0])
    pj_own = pltpu.make_async_copy(proj_ref, PJ, loc_sem.at[2])
    pj_own.start()
    m_own = [pltpu.make_async_copy(m1_ref, M1, loc_sem.at[3]), pltpu.make_async_copy(m2_ref, M2, loc_sem.at[4])]
    for cp in m_own:
        cp.start()
    tok_own.start()

    def og_src(par, cls, yl_, z_):
        return grad_ref.at[:, pl.ds(pl.multiple_of(z_ * 1024 + yl_ * 512 + par * 256 + cls * 128, 128), 128)]

    def og_dst(cls, yl_, z_):
        return OG.at[c, cls, yl_, z_ // ZC, :, pl.ds((z_ % ZC) * 128, 128)]

    for cls in range(2):
        for yl_ in range(2):
            for z_ in range(NZ):
                pltpu.make_async_copy(og_src(c, cls, yl_, z_), og_dst(cls, yl_, z_), loc_sem.at[1]).start()

    pj_own.wait()
    for h in range(2):
        for cls in range(2):
            S[h, cls] = PJ[:, h * 256 + cls * 128:h * 256 + cls * 128 + 128]
    pl.semaphore_wait(barrier, len(peers))

    W[:, yh, x, z, yl, pl.ds(pl.multiple_of(c * 32, 32), 32), :] = S[c]
    z_order = (0, 1, 7, 2, 6, 3, 5, 4)
    for k in z_order:
        for rel in range(2):
            if k == 0 and rel == 0:
                continue
            t = c if rel == 0 else 1 - c
            cp = rcopy(S.at[t], W.at[:, yh, x, z, yl, pl.ds(pl.multiple_of(c * 32, 32), 32)],
                       snd.at[0], zr.at[k], dev(x, y, zp(k), t))
            cp.start()


    def proj_step(k):
        w0 = W[0, k // 4, lax.rem(k, 4)].reshape(1024, 128)
        w1 = W[1, k // 4, lax.rem(k, 4)].reshape(1024, 128)
        w = jnp.concatenate([w0, w1], axis=1)
        tk = T[:, :, pl.ds(pl.multiple_of(k * 1024, 1024), 1024)].reshape(512, 1024)
        ACC[...] += jnp.dot(tk, w, preferred_element_type=F32)
        return 0


    def line(cls, k):
        return dev(x, yp(k), z, c) if cls == 0 else dev(xp(k), y, z, c)

    def block(cls, j, k, zs_):
        xb = lax.rem(x + NX - (j if cls == 0 else k), NX)
        yb = lax.rem(y + NY - (k if cls == 0 else j), NY)
        return W.at[cls, yb // 2, xb, zs_, lax.rem(yb, 2)]

    whole_z, low_z, high_z = pl.ds(0, NZ), pl.ds(0, NZ // 2), pl.ds(NZ // 2, NZ // 2)

    def send(cls, j, key, blk, k):
        rcopy(blk, blk, snd.at[1], fr.at[cls, j, key], line(cls, k)).start()

    def forward(cls, j):
        for k in (1, 3):
            send(cls, j, k // 2, block(cls, j, 0, whole_z), k)

    def relay(cls, j):
        arrived(16, 4096, fr.at[cls, j, 0])
        send(cls, j, 2, block(cls, j, 1, low_z), 1)
        arrived(16, 4096, fr.at[cls, j, 1])
        send(cls, j, 2, block(cls, j, 3, high_z), 3)

    for k in z_order:
        arrived(16, 512 if k == 0 else 1024, zr.at[k])
        for cls in range(2):
            blk = W.at[cls, yh, x, lax.rem(z + NZ - k, NZ), yl]
            for m in (1, 3, 2):
                to = dev(xp(m), y, z, c) if cls == 0 else dev(x, yp(m), z, c)
                rcopy(blk, blk, snd.at[2], mr.at[cls, m], to).start()
            for m in (1, 3):
                send(cls, 0, m // 2, blk, m)

    tok_ex = rcopy(tok_ref, T.at[c], ex_s.at[0], ex_r.at[0], sib)
    tok_ex.start()
    for cls in range(2):
        for yl_ in range(2):
            for z_ in range(NZ):
                rcopy(og_src(1 - c, cls, yl_, z_), og_dst(cls, yl_, z_), ex_s.at[1], ex_r.at[1], sib).start()
    og_ex = rcopy(OG.at[c], OG.at[1 - c], ex_s.at[1], ex_r.at[1], sib)

    for j in (1, 3, 2):
        for cls in range(2):
            arrived(16, 4096, mr.at[cls, j])
            forward(cls, j)
        for cls in range(2):
            relay(cls, 0 if j == 1 else 1 if j == 3 else 3)
    for cls in range(2):
        relay(cls, 2)
    tok_own.wait()
    tok_ex.wait()
    ACC[...] = jnp.zeros_like(ACC)
    for j in (0, 1, 3):
        for cls in range(2):
            arrived(16, 4096, fr.at[cls, j, 2])
    lax.fori_loop(0, 3, lambda i, _: proj_step(yh * 4 + lax.rem(x + 3 + i, NX)), 0)
    for cls in range(2):
        arrived(16, 4096, fr.at[cls, 2, 2])

    lr_copy = rcopy(W.at[:, yh, x], LR, lr_sem.at[0], lr_sem.at[1], sib)
    lr_copy.start()
    proj_step(yh * 4 + lax.rem(x + 2, NX))
    lax.fori_loop(0, 4, lambda i, _: proj_step((1 - yh) * 4 + i), 0)
    PJT[c] = ACC[...].T.astype(BF)
    pj_copy = rcopy(PJT.at[c], PJT.at[c], pj_sem.at[0], pj_sem.at[1], sib)
    pj_copy.start()
    pltpu.make_async_copy(OG.at[c], OG.at[c], loc_sem.at[1]).wait()
    og_ex.wait()

    def chunk(j):
        return lax.rem(z // ZC + 1 + j, NCH)

    def part(j, r):
        def part_step(i, _):
            cls, yl_ = i // 2, lax.rem(i, 2)
            v = jnp.dot(PJT[r, :, 0:256], OG[0, cls, yl_, chunk(j)], preferred_element_type=F32)
            v = v + jnp.dot(PJT[r, :, 256:512], OG[1, cls, yl_, chunk(j)], preferred_element_type=F32)
            PF[cls, j, yl_, r] = v.reshape(4, 64, CW)
            PT[cls, j, yl_, r] = v.astype(BF).reshape(4, 64, CW)
            return 0

        lax.fori_loop(0, 4, part_step, 0, unroll=True)

    KD = (1, 3)

    def half(ref, cls, j, k, h):
        if cls == 0:
            q = yp(k)
            return ref.at[0, j, lax.rem(q, 2), q // 2, 2 * h:2 * h + 2]
        return ref.at[1, j, h, :, xp(k)]

    relays = {}

    def send_partials(j):
        for cls in range(2):
            for d in range(2):
                cp = rcopy(half(PT, cls, j, 2, d), RL.at[cls, j, d], snd.at[3], r1.at[cls, j, d], line(cls, KD[d]))
                cp.start()
                relays[cls, j, d] = cp
        for cls in range(2):
            for d in range(2):
                rcopy(half(PT, cls, j, KD[d], 1 - d), R1.at[j, cls, d, 1 - d], snd.at[3], rf.at[j],
                      line(cls, KD[d])).start()

    def relay_partials(j):
        for d in range(2):
            for cls in range(2):
                relays[cls, j, d].wait_recv()
                AGB[cls, j, d] = (half(PF, cls, j, KD[d], d)[...] + RL[cls, j, d].astype(F32)).astype(BF)
                rcopy(AGB.at[cls, j, d], R1.at[j, cls, d, d], snd.at[4], rf.at[j], line(cls, KD[d])).start()

    def first_sums(j):
        arrived(32, 8192, rf.at[j])
        for h in range(2):
            SB[j, 2 * h:2 * h + 2] = half(PF, 0, j, 0, h)[...] + R1[j, 0, 0, h].astype(F32) + R1[j, 0, 1, h].astype(F32)
            SC[j, h] = half(PF, 1, j, 0, h)[...] + R1[j, 1, 0, h].astype(F32) + R1[j, 1, 1, h].astype(F32)
        for k in (2, 1, 3):
            q = yp(k)
            rcopy(SB.at[j, xp(k)], R2.at[j, 0, k - 1], snd.at[5], r2.at[j], dev(xp(k), y, z, c)).start()
            rcopy(SC.at[j, lax.rem(q, 2), q // 2], R2.at[j, 1, k - 1], snd.at[5], r2.at[j], dev(x, q, z, c)).start()

    def second_sums(j):
        arrived(48, 4096, r2.at[j])
        vb = SB[j, x] + R2[j, 0, 0] + R2[j, 0, 1] + R2[j, 0, 2]
        vc = SC[j, yl, yh] + R2[j, 1, 0] + R2[j, 1, 1] + R2[j, 1, 2]
        for i in range(ZC):
            to = chunk(j) * ZC + i
            T3[to, 0] = vb[:, i * 128:(i + 1) * 128]
            T3[to, 1] = vc[:, i * 128:(i + 1) * 128]

            @pl.when(to != z)
            def _(to=to):
                rcopy(T3.at[to], R3.at[z], snd.at[6], rcv.at[2], dev(x, y, to, c)).start()

    for step in range(NCH + 3):
        if step < NCH:
            part(step, c)
            if step == 0:
                pj_copy.wait()
            part(step, 1 - c)
            send_partials(step)
        if 0 <= step - 1 < NCH:
            relay_partials(step - 1)
        if 0 <= step - 2 < NCH:
            first_sums(step - 2)
        if 0 <= step - 3 < NCH:
            second_sums(step - 3)

    R3[z] = T3[z]
    arrived(112, 2048, rcv.at[2])

    g0 = R3[0]
    for k in range(1, NZ):
        g0 = g0 + R3[k]
    g = jnp.concatenate([g0[0], g0[1]], axis=1)
    for cp in m_own:
        cp.wait()
    first = beta_one * M1[...] + (1.0 - beta_one) * g
    second = beta_two * M2[...] + (1.0 - beta_two) * g * g
    o1_ref[...] = first
    o2_ref[...] = second
    D[dp] = (first / (jnp.sqrt(second) + adam_epsilon)).astype(BF)
    for k in range(1, 8):
        q = lax.rem(dp + k, 8)
        rcopy(D.at[dp], D.at[dp], snd.at[7], rcv.at[3], (q, sh)).start()
    arrived(240, 512, snd.at[0])
    arrived(192, 8192, snd.at[1])
    arrived(48, 8192, snd.at[2])
    arrived(128, 8192, snd.at[3])
    arrived(64, 8192, snd.at[4])
    arrived(96, 8192, snd.at[5])
    arrived(112, 2048, snd.at[6])
    lr_copy.wait()
    arrived(112, 1024, rcv.at[3])
    arrived(112, 1024, snd.at[7])
    d_own = D[pl.ds(c * 4, 4)].reshape(256, 256)
    d_sib = D[pl.ds((1 - c) * 4, 4)].reshape(256, 256)
    for b in range(4):
        own = jnp.concatenate([W[h, yh, x, 2 * b:2 * b + 2].reshape(256, 128) for h in range(2)], axis=1)
        oth = jnp.concatenate([LR[h, 2 * b:2 * b + 2].reshape(256, 128) for h in range(2)], axis=1)
        u = jnp.dot(own, d_own, preferred_element_type=F32) + jnp.dot(oth, d_sib, preferred_element_type=F32)
        up_ref[b * 256:(b + 1) * 256, :] = u.astype(BF)


def store_outputs(a_ref, b_ref, u_ref, ao_ref, bo_ref, uo_ref, sem):
    copies = [
        pltpu.make_async_copy(u_ref, uo_ref, sem.at[0]),
        pltpu.make_async_copy(a_ref, ao_ref, sem.at[1]),
        pltpu.make_async_copy(b_ref, bo_ref, sem.at[2]),
    ]
    for cp in copies:
        cp.start()
    for cp in copies:
        cp.wait()


def on_device(tokens, out_grad, projector, first_moment, second_moment):
    vm = pl.BlockSpec(memory_space=pltpu.VMEM)
    hbm = pl.BlockSpec(memory_space=pl.ANY)
    dma = pltpu.SemaphoreType.DMA
    held = pl.pallas_call(
        kernel,
        out_shape=(pltpu.VMEM((64, 256), F32), pltpu.VMEM((64, 256), F32), pltpu.VMEM((1024, 256), BF)),
        in_specs=[pl.BlockSpec(memory_space=pltpu.HBM)] * 5,
        out_specs=(vm, vm, vm),
        scratch_shapes=[
            pltpu.VMEM((2, 256, 8192), BF),
            pltpu.VMEM((2, 2, 2, NCH, 256, CW), BF),
            pltpu.VMEM((32, 512), BF),
            pltpu.VMEM((64, 256), F32),
            pltpu.VMEM((64, 256), F32),
            pltpu.VMEM((2, 2, 32, 128), BF),
            pltpu.VMEM((2, 2, 4, 8, 2, 64, 128), BF),
            pltpu.VMEM((2, 8, 2, 64, 128), BF),
            pltpu.VMEM((512, 256), F32),
            pltpu.VMEM((2, 256, 512), BF),
            pltpu.VMEM((2, NCH, 2, 2, 4, 64, CW), BF),
            pltpu.VMEM((2, NCH, 2, 2, 4, 64, CW), F32),
            pltpu.VMEM((2, NCH, 2, 2, 64, CW), BF),
            pltpu.VMEM((2, NCH, 2, 2, 64, CW), BF),
            pltpu.VMEM((NCH, 2, 2, 2, 2, 64, CW), BF),
            pltpu.VMEM((NCH, 4, 64, CW), F32),
            pltpu.VMEM((NCH, 2, 2, 64, CW), F32),
            pltpu.VMEM((NCH, 2, 3, 64, CW), F32),
            pltpu.VMEM((8, 2, 64, 128), F32),
            pltpu.VMEM((8, 2, 64, 128), F32),
            pltpu.VMEM((8, 64, 256), BF),
            dma((5,)), dma((2,)), dma((2,)),
            dma((8,)), dma((2, 4)), dma((2, 4, 3)),
            dma((2,)), dma((2,)),
            dma((2, NCH, 2)), dma((NCH,)), dma((NCH,)),
            dma((8,)), dma((4,)),
        ],
        compiler_params=pltpu.CompilerParams(
            collective_id=0, has_side_effects=True, vmem_limit_bytes=56 * 2**20
        ),
        name="galore",
    )(tokens, out_grad, projector, first_moment, second_moment)
    return pl.pallas_call(
        store_outputs,
        out_shape=(
            jax.ShapeDtypeStruct((64, 256), F32),
            jax.ShapeDtypeStruct((64, 256), F32),
            jax.ShapeDtypeStruct((1024, 256), BF),
        ),
        in_specs=[vm, vm, vm],
        out_specs=(hbm, hbm, hbm),
        scratch_shapes=[dma((3,))],
        name="store_outputs",
    )(*[pltpu.with_memory_space_constraint(a, pltpu.VMEM) for a in held])


def solution(mesh):
    in_specs = (
        P(("dp", "shard"), None),
        P(("dp", "shard"), None),
        P(("dp", "shard"), None),
        P("dp", "shard"),
        P("dp", "shard"),
    )
    out_specs = (P("dp", "shard"), P("dp", "shard"), P("dp", "shard"))
    return jax.shard_map(
        on_device, mesh=mesh, in_specs=in_specs, out_specs=out_specs, check_vma=False
    )
```

time: 761 us -> 90.8 us (0.12)
  waiting for transfers between devices: 692 us -> 0 us
  Pallas kernels: 0 us -> 90 us
  blocking collectives: 34.4 us -> 0 us
  matrix products: 18.6 us -> 0 us
  between operations: 13.8 us -> 0.64 us
    all_gather x1 -> x0, waiting for transfers between devices: 425 us -> none  [on_device(): whole = lax.all_gather(projector, ('dp', 'shard'), axis=0, tiled=True)]
    reduce_scatter x2 -> x0, waiting for transfers between devices: 267 us -> none  [the longest x1 183 us: on_device(): lax.psum_scatter(partial_value, 'shard', scatter_dimension=1, tiled=True)]
    pallas_call x0 -> x2, Pallas kernels: none -> 90 us  [the longest x1 89.2 us: on_device(): pl.pallas_call(kernel, out_shape=(pltpu.VMEM((64, 256), F32), pltpu.VMEM(...]
    all_gather x1 -> x0, blocking collectives: 34.4 us -> none  [on_device(): lax.all_gather(direction, 'dp', axis=0, tiled=True)]
    dot_general x2 -> x0, matrix products: 18.6 us -> none  [the longest x1 16.2 us: on_device(): lax.dot_general(projected, out_grad, (((0,), (0,)), ((), ())), preferred_...]
  transfers between devices with their start and end apart: 3 -> 0, of which waited for: 3 -> 0; matrix products, arithmetic and copies ran while one was open for 0% -> 0% of each run, Pallas kernels for 0% -> 0%
where the time goes in v2:
time: 90.8 us; the launch traced here: 90.7 us
  Pallas kernels  90 us (99%)
    pallas_call x1, Pallas kernels, on_device(): pl.pallas_call(kernel, out_shape=(pltpu.VMEM((64, 256), F32), pltpu.VMEM(...  89.2 us

profile of v2, /device:TPU:32, one launch (start us, length us, event | category | flops | bytes accessed | tf_op | source)
XLA Modules:
  0.0 90.7 jit_solution(9509044292189544564)
XLA Ops:
  0.6 89.2 %galore.1 = (f32[64,256]{1,0:T(8,128)S(1)}, f32[64,256]{1,0:T(8,128)S(1)}, bf16[1024,256]{1,0:T(8,128)(2,1)S(1)}) custom-call(bf16[256,8192]{1,0:T(8,128)(2,1)} %tok_ref.1, bf16[256,8192]{1,0:T(8,128)(2,1)} %grad_ref.1, bf16[32,512]{1,0:T(8,128)(2,1)} %proj_ref.1, f32[64,256]{1,0:T(8,128)} %m1_ref.1, f32[64,256]{1,0:T(8,128)} %m2_ref.1), custom_call_target="tpu_custom_call" | custom-call | tf_op jit(solution)/shard_map/galore/pallas_call | solution.py:306
  89.8 0.9 store_outputs.1

commit v3 on v2

--- a/solution.py
+++ b/solution.py
@@ -18,7 +18,7 @@
 
 
 def kernel(tok_ref, grad_ref, proj_ref, m1_ref, m2_ref, o1_ref, o2_ref, up_ref,
-           T, OG, PJ, M1, M2, S, W, LR, ACC, PJT, PT, PF, RL, AGB, R1, SB, SC, R2, T3, R3, D,
+           T, OG, OGX, PJX, PJ, M1, M2, S, W, LR, ACC, PJT, PT, PF, RL, AGB, R1, SB, SC, R2, T3, R3, D,
            loc_sem, ex_s, ex_r, zr, mr, fr, lr_sem, pj_sem, r1, rf, r2, snd, rcv):
     dp = lax.axis_index("dp")
     sh = lax.axis_index("shard")
@@ -39,6 +39,11 @@
         return lax.rem(z + k, NZ)
 
     sib = dev(x, y, z, 1 - c)
+    p = lax.rem(z, 2)
+    zq = z + 1 - 2 * p
+
+    def chunk(j):
+        return lax.rem(z // ZC + 1 + j, NCH)
 
     def arrived(rows, columns, sem):
         ref = T.at[0, 0:rows, 0:columns]
@@ -54,8 +59,8 @@
         peers += [dev(x, y, zp(k), c), dev(x, y, zp(k), 1 - c)]
     for k in range(1, 4):
         peers += [dev(xp(k), y, z, c), dev(x, yp(k), z, c), dev(xp(k), yp(2), z, c)]
-    for p in peers:
-        pl.semaphore_signal(barrier, inc=1, device_id=p, device_id_type=MESH)
+    for peer in peers:
+        pl.semaphore_signal(barrier, inc=1, device_id=peer, device_id_type=MESH)
 
     tok_own = pltpu.make_async_copy(tok_ref, T.at[c], loc_sem.at[0])
     pj_own = pltpu.make_async_copy(proj_ref, PJ, loc_sem.at[2])
@@ -143,6 +148,12 @@
             for z_ in range(NZ):
                 rcopy(og_src(1 - c, cls, yl_, z_), og_dst(cls, yl_, z_), ex_s.at[1], ex_r.at[1], sib).start()
     og_ex = rcopy(OG.at[c], OG.at[1 - c], ex_s.at[1], ex_r.at[1], sib)
+    for jj in range(2):
+        for cls in range(2):
+            for yl_ in range(2):
+                for c_ in range(2):
+                    rcopy(og_src(c_, cls, yl_, chunk(2 + jj) * ZC + 1 - p), OGX.at[c, cls, yl_, jj],
+                          snd.at[8], rcv.at[0], dev(x, y, zq, c_)).start()
 
     for j in (1, 3, 2):
         for cls in range(2):
@@ -169,93 +180,133 @@
     PJT[c] = ACC[...].T.astype(BF)
     pj_copy = rcopy(PJT.at[c], PJT.at[c], pj_sem.at[0], pj_sem.at[1], sib)
     pj_copy.start()
+    pjx_copy = rcopy(PJT.at[c], PJX.at[c], snd.at[9], pj_sem.at[2], dev(x, y, zq, c))
+    pjx_copy.start()
     pltpu.make_async_copy(OG.at[c], OG.at[c], loc_sem.at[1]).wait()
     og_ex.wait()
 
-    def chunk(j):
-        return lax.rem(z // ZC + 1 + j, NCH)
-
     def part(j, r):
+        def product(t, cls, yl_):
+            lhs = (PJT if t < 2 else PJX)[r, :, (t % 2) * 256:(t % 2) * 256 + 256]
+            if t >= 2:
+                rhs = OGX[t - 2, cls, yl_, j - 2]
+            elif j < 2:
+                rhs = OG[t, cls, yl_, chunk(j)]
+            else:
+                rhs = OG[t, cls, yl_, chunk(j), :, pl.ds(pl.multiple_of(p * 128, 128), 128)]
+            return jnp.dot(lhs, rhs, preferred_element_type=F32)
+
         def part_step(i, _):
             cls, yl_ = i // 2, lax.rem(i, 2)
-            v = jnp.dot(PJT[r, :, 0:256], OG[0, cls, yl_, chunk(j)], preferred_element_type=F32)
-            v = v + jnp.dot(PJT[r, :, 256:512], OG[1, cls, yl_, chunk(j)], preferred_element_type=F32)
-            PF[cls, j, yl_, r] = v.reshape(4, 64, CW)
-            PT[cls, j, yl_, r] = v.astype(BF).reshape(4, 64, CW)
+            v = product(0, cls, yl_) + product(1, cls, yl_)
+            if j >= 2:
+                v = v + product(2, cls, yl_) + product(3, cls, yl_)
+            PF[cls, j, yl_, r, :, :, 0:width(j)] = v.reshape(4, 64, width(j))
+            PT[cls, j, yl_, r, :, :, 0:width(j)] = v.astype(BF).reshape(4, 64, width(j))
             return 0
 
         lax.fori_loop(0, 4, part_step, 0, unroll=True)
+
+    def width(j):
+        return CW if j < 2 else 128
 
     KD = (1, 3)
 
     def half(ref, cls, j, k, h):
         if cls == 0:
             q = yp(k)
-            return ref.at[0, j, lax.rem(q, 2), q // 2, 2 * h:2 * h + 2]
-        return ref.at[1, j, h, :, xp(k)]
+            return ref.at[0, j, lax.rem(q, 2), q // 2, 2 * h:2 * h + 2, :, 0:width(j)]
+        return ref.at[1, j, h, :, xp(k), :, 0:width(j)]
 
     relays = {}
 
     def send_partials(j):
         for cls in range(2):
             for d in range(2):
-                cp = rcopy(half(PT, cls, j, 2, d), RL.at[cls, j, d], snd.at[3], r1.at[cls, j, d], line(cls, KD[d]))
+                cp = rcopy(half(PT, cls, j, 2, d), RL.at[cls, j, d, :, :, 0:width(j)], snd.at[3],
+                           r1.at[cls, j, d], line(cls, KD[d]))
                 cp.start()
                 relays[cls, j, d] = cp
         for cls in range(2):
             for d in range(2):
-                rcopy(half(PT, cls, j, KD[d], 1 - d), R1.at[j, cls, d, 1 - d], snd.at[3], rf.at[j],
-                      line(cls, KD[d])).start()
+                rcopy(half(PT, cls, j, KD[d], 1 - d), R1.at[j, cls, d, 1 - d, :, :, 0:width(j)], snd.at[3],
+                      rf.at[j], line(cls, KD[d])).start()
 
     def relay_partials(j):
+        w = width(j)
         for d in range(2):
             for cls in range(2):
                 relays[cls, j, d].wait_recv()
-                AGB[cls, j, d] = (half(PF, cls, j, KD[d], d)[...] + RL[cls, j, d].astype(F32)).astype(BF)
-                rcopy(AGB.at[cls, j, d], R1.at[j, cls, d, d], snd.at[4], rf.at[j], line(cls, KD[d])).start()
+                both = half(PF, cls, j, KD[d], d)[...] + RL[cls, j, d, :, :, 0:w].astype(F32)
+                AGB[cls, j, d, :, :, 0:w] = both.astype(BF)
+                rcopy(AGB.at[cls, j, d, :, :, 0:w], R1.at[j, cls, d, d, :, :, 0:w], snd.at[4], rf.at[j],
+                      line(cls, KD[d])).start()
 
     def first_sums(j):
-        arrived(32, 8192, rf.at[j])
+        w = width(j)
+        arrived(w // 8, 8192, rf.at[j])
+
+        def total(cls, h):
+            v = half(PF, cls, j, 0, h)[...]
+            for d in range(2):
+                v = v + R1[j, cls, d, h, :, :, 0:w].astype(F32)
+            return v
+
         for h in range(2):
-            SB[j, 2 * h:2 * h + 2] = half(PF, 0, j, 0, h)[...] + R1[j, 0, 0, h].astype(F32) + R1[j, 0, 1, h].astype(F32)
-            SC[j, h] = half(PF, 1, j, 0, h)[...] + R1[j, 1, 0, h].astype(F32) + R1[j, 1, 1, h].astype(F32)
+            SB[j, 2 * h:2 * h + 2, :, 0:w] = total(0, h)
+            SC[j, h, :, :, 0:w] = total(1, h)
         for k in (2, 1, 3):
             q = yp(k)
-            rcopy(SB.at[j, xp(k)], R2.at[j, 0, k - 1], snd.at[5], r2.at[j], dev(xp(k), y, z, c)).start()
-            rcopy(SC.at[j, lax.rem(q, 2), q // 2], R2.at[j, 1, k - 1], snd.at[5], r2.at[j], dev(x, q, z, c)).start()
+            rcopy(SB.at[j, xp(k), :, 0:w], R2.at[j, 0, k - 1, :, 0:w], snd.at[5], r2.at[j],
+                  dev(xp(k), y, z, c)).start()
+            rcopy(SC.at[j, lax.rem(q, 2), q // 2, :, 0:w], R2.at[j, 1, k - 1, :, 0:w], snd.at[5], r2.at[j],
+                  dev(x, q, z, c)).start()
 
     def second_sums(j):
-        arrived(48, 4096, r2.at[j])
-        vb = SB[j, x] + R2[j, 0, 0] + R2[j, 0, 1] + R2[j, 0, 2]
-        vc = SC[j, yl, yh] + R2[j, 1, 0] + R2[j, 1, 1] + R2[j, 1, 2]
-        for i in range(ZC):
-            to = chunk(j) * ZC + i
-            T3[to, 0] = vb[:, i * 128:(i + 1) * 128]
-            T3[to, 1] = vc[:, i * 128:(i + 1) * 128]
-
-            @pl.when(to != z)
-            def _(to=to):
-                rcopy(T3.at[to], R3.at[z], snd.at[6], rcv.at[2], dev(x, y, to, c)).start()
+        w = width(j)
+        arrived(48, w * 16, r2.at[j])
+        vb = SB[j, x, :, 0:w]
+        vc = SC[j, yl, yh, :, 0:w]
+        for k in range(3):
+            vb = vb + R2[j, 0, k, :, 0:w]
+            vc = vc + R2[j, 1, k, :, 0:w]
+        if j == NCH - 1:
+            R3[5, 0] = vb
+            R3[5, 1] = vc
+            return
+        for i in range(w // 128):
+            slot = 2 * j + i
+            T3[slot, 0] = vb[:, i * 128:(i + 1) * 128]
+            T3[slot, 1] = vc[:, i * 128:(i + 1) * 128]
+            to = chunk(j) * ZC + (i if j < 2 else p)
+            rcopy(T3.at[slot], R3.at[2 * j + (p if j < 2 else 0)], snd.at[6], rcv.at[2], dev(x, y, to, c)).start()
 
     for step in range(NCH + 3):
         if step < NCH:
+            if step == 2:
+                pjx_copy.wait_recv()
+                pjx_on = rcopy(PJX.at[c], PJX.at[c], snd.at[9], pj_sem.at[3], sib)
+                pjx_on.start()
+                arrived(64, 8192, rcv.at[0])
             part(step, c)
             if step == 0:
                 pj_copy.wait()
+            if step == 2:
+                pjx_on.wait_recv()
             part(step, 1 - c)
             send_partials(step)
-        if 0 <= step - 1 < NCH:
+        if step in (1, 2, 3):
             relay_partials(step - 1)
-        if 0 <= step - 2 < NCH:
+        if step in (2, 3, 4, 5):
             first_sums(step - 2)
-        if 0 <= step - 3 < NCH:
+        if step == 3:
+            relay_partials(3)
+        if step in (3, 4, 5, 6):
             second_sums(step - 3)
 
-    R3[z] = T3[z]
-    arrived(112, 2048, rcv.at[2])
-
+    arrived(80, 2048, rcv.at[2])
     g0 = R3[0]
-    for k in range(1, NZ):
+    for k in range(1, 6):
         g0 = g0 + R3[k]
     g = jnp.concatenate([g0[0], g0[1]], axis=1)
     for cp in m_own:
@@ -265,16 +316,18 @@
     o1_ref[...] = first
     o2_ref[...] = second
     D[dp] = (first / (jnp.sqrt(second) + adam_epsilon)).astype(BF)
-    for k in range(1, 8):
-        q = lax.rem(dp + k, 8)
+    for dx, dy in ((2, 1), (1, 1), (3, 1), (2, 0), (0, 1), (1, 0), (3, 0)):
+        q = lax.rem(yh + dy, 2) * 4 + xp(dx)
         rcopy(D.at[dp], D.at[dp], snd.at[7], rcv.at[3], (q, sh)).start()
     arrived(240, 512, snd.at[0])
     arrived(192, 8192, snd.at[1])
     arrived(48, 8192, snd.at[2])
-    arrived(128, 8192, snd.at[3])
-    arrived(64, 8192, snd.at[4])
-    arrived(96, 8192, snd.at[5])
-    arrived(112, 2048, snd.at[6])
+    arrived(96, 8192, snd.at[3])
+    arrived(48, 8192, snd.at[4])
+    arrived(144, 4096, snd.at[5])
+    arrived(80, 2048, snd.at[6])
+    arrived(64, 8192, snd.at[8])
+    arrived(32, 8192, snd.at[9])
     lr_copy.wait()
     arrived(112, 1024, rcv.at[3])
     arrived(112, 1024, snd.at[7])
@@ -311,6 +364,8 @@
         scratch_shapes=[
             pltpu.VMEM((2, 256, 8192), BF),
             pltpu.VMEM((2, 2, 2, NCH, 256, CW), BF),
+            pltpu.VMEM((2, 2, 2, 2, 256, 128), BF),
+            pltpu.VMEM((2, 256, 512), BF),
             pltpu.VMEM((32, 512), BF),
             pltpu.VMEM((64, 256), F32),
             pltpu.VMEM((64, 256), F32),
@@ -327,14 +382,14 @@
             pltpu.VMEM((NCH, 4, 64, CW), F32),
             pltpu.VMEM((NCH, 2, 2, 64, CW), F32),
             pltpu.VMEM((NCH, 2, 3, 64, CW), F32),
-            pltpu.VMEM((8, 2, 64, 128), F32),
-            pltpu.VMEM((8, 2, 64, 128), F32),
+            pltpu.VMEM((5, 2, 64, 128), F32),
+            pltpu.VMEM((6, 2, 64, 128), F32),
             pltpu.VMEM((8, 64, 256), BF),
             dma((5,)), dma((2,)), dma((2,)),
             dma((8,)), dma((2, 4)), dma((2, 4, 3)),
-            dma((2,)), dma((2,)),
+            dma((2,)), dma((4,)),
             dma((2, NCH, 2)), dma((NCH,)), dma((NCH,)),
-            dma((8,)), dma((4,)),
+            dma((10,)), dma((4,)),
         ],
         compiler_params=pltpu.CompilerParams(
             collective_id=0, has_side_effects=True, vmem_limit_bytes=56 * 2**20

time: 90.8 us -> 83.8 us (0.923)
  Pallas kernels: 90 us -> 82.6 us
    pallas_call x1, Pallas kernels: 89.2 us -> 81.8 us  [on_device(): pl.pallas_call(kernel, out_shape=(pltpu.VMEM((64, 256), F32), pltpu.VMEM(...]
where the time goes in v3:
time: 83.8 us; the launch traced here: 83.2 us
  Pallas kernels  82.6 us (99%)
    pallas_call x1, Pallas kernels, on_device(): pl.pallas_call(kernel, out_shape=(pltpu.VMEM((64, 256), F32), pltpu.VMEM(...  81.8 us

profile of v3, /device:TPU:32, one launch (start us, length us, event | category | flops | bytes accessed | tf_op | source)
XLA Modules:
  0.0 83.2 jit_solution(7245519232634670359)
XLA Ops:
  0.6 81.8 %galore.1 = (f32[64,256]{1,0:T(8,128)S(1)}, f32[64,256]{1,0:T(8,128)S(1)}, bf16[1024,256]{1,0:T(8,128)(2,1)S(1)}) custom-call(bf16[256,8192]{1,0:T(8,128)(2,1)} %tok_ref.1, bf16[256,8192]{1,0:T(8,128)(2,1)} %grad_ref.1, bf16[32,512]{1,0:T(8,128)(2,1)} %proj_ref.1, f32[64,256]{1,0:T(8,128)} %m1_ref.1, f32[64,256]{1,0:T(8,128)} %m2_ref.1), custom_call_target="tpu_custom_call" | custom-call | tf_op jit(solution)/shard_map/galore/pallas_call | solution.py:359
  82.4 0.9 %store_outputs.1 = (f32[64,256]{1,0:T(8,128)}, f32[64,256]{1,0:T(8,128)}, bf16[1024,256]{1,0:T(8,128)(2,1)}) custom-call(f32[64,256]{1,0:T(8,128)S(1)} %get-tuple-element.6.a_ref, f32[64,256]{1,0:T(8,128)S(1)} %get-tuple-element.7.b_ref, bf16[1024,256]{1,0:T(8,128)(2,1)S(1)} %get-tuple-element.8.u_ref), custom_call_target="tpu_custom_call" | custom-call | tf_op jit(solution)/shard_map/store_outputs/pallas_call | solution.py:399

commit v4 on v3

--- a/solution.py
+++ b/solution.py
@@ -18,7 +18,7 @@
 
 
 def kernel(tok_ref, grad_ref, proj_ref, m1_ref, m2_ref, o1_ref, o2_ref, up_ref,
-           T, OG, OGX, PJX, PJ, M1, M2, S, W, LR, ACC, PJT, PT, PF, RL, AGB, R1, SB, SC, R2, T3, R3, D,
+           T, OG, OGX, PJX, PJ, M1, M2, S, W, LR, U, ACC, PJT, PT, PF, RL, AGB, R1, SB, SC, R2, T3, R3, D,
            loc_sem, ex_s, ex_r, zr, mr, fr, lr_sem, pj_sem, r1, rf, r2, snd, rcv):
     dp = lax.axis_index("dp")
     sh = lax.axis_index("shard")
@@ -43,7 +43,7 @@
     zq = z + 1 - 2 * p
 
     def chunk(j):
-        return lax.rem(z // ZC + 1 + j, NCH)
+        return lax.rem(z // ZC + (1, 3, 2, 0)[j], NCH)
 
     def arrived(rows, columns, sem):
         ref = T.at[0, 0:rows, 0:columns]
@@ -173,8 +173,10 @@
     for cls in range(2):
         arrived(16, 4096, fr.at[cls, 2, 2])
 
-    lr_copy = rcopy(W.at[:, yh, x], LR, lr_sem.at[0], lr_sem.at[1], sib)
+    lr_copy = rcopy(W.at[:, yh, x], LR.at[c], lr_sem.at[0], lr_sem.at[1], sib)
     lr_copy.start()
+    lr_own = pltpu.make_async_copy(W.at[:, yh, x], LR.at[c], loc_sem.at[5])
+    lr_own.start()
     proj_step(yh * 4 + lax.rem(x + 2, NX))
     lax.fori_loop(0, 4, lambda i, _: proj_step((1 - yh) * 4 + i), 0)
     PJT[c] = ACC[...].T.astype(BF)
@@ -281,28 +283,36 @@
             to = chunk(j) * ZC + (i if j < 2 else p)
             rcopy(T3.at[slot], R3.at[2 * j + (p if j < 2 else 0)], snd.at[6], rcv.at[2], dev(x, y, to, c)).start()
 
-    for step in range(NCH + 3):
-        if step < NCH:
-            if step == 2:
-                pjx_copy.wait_recv()
-                pjx_on = rcopy(PJX.at[c], PJX.at[c], snd.at[9], pj_sem.at[3], sib)
-                pjx_on.start()
-                arrived(64, 8192, rcv.at[0])
-            part(step, c)
-            if step == 0:
-                pj_copy.wait()
-            if step == 2:
-                pjx_on.wait_recv()
-            part(step, 1 - c)
-            send_partials(step)
-        if step in (1, 2, 3):
-            relay_partials(step - 1)
-        if step in (2, 3, 4, 5):
-            first_sums(step - 2)
-        if step == 3:
-            relay_partials(3)
-        if step in (3, 4, 5, 6):
-            second_sums(step - 3)
+    def partials(j):
+        if j == 2:
+            pjx_copy.wait_recv()
+            pjx_on = rcopy(PJX.at[c], PJX.at[c], snd.at[9], pj_sem.at[3], sib)
+            pjx_on.start()
+            arrived(64, 8192, rcv.at[0])
+        part(j, c)
+        if j == 0:
+            pj_copy.wait()
+        if j == 2:
+            pjx_on.wait_recv()
+        part(j, 1 - c)
+        send_partials(j)
+
+    partials(0)
+    partials(1)
+    relay_partials(0)
+    partials(2)
+    relay_partials(1)
+    first_sums(0)
+    partials(3)
+    relay_partials(2)
+    first_sums(1)
+    second_sums(0)
+    relay_partials(3)
+    first_sums(2)
+    second_sums(1)
+    first_sums(3)
+    second_sums(2)
+    second_sums(3)
 
     arrived(80, 2048, rcv.at[2])
     g0 = R3[0]
@@ -318,7 +328,7 @@
     D[dp] = (first / (jnp.sqrt(second) + adam_epsilon)).astype(BF)
     for dx, dy in ((2, 1), (1, 1), (3, 1), (2, 0), (0, 1), (1, 0), (3, 0)):
         q = lax.rem(yh + dy, 2) * 4 + xp(dx)
-        rcopy(D.at[dp], D.at[dp], snd.at[7], rcv.at[3], (q, sh)).start()
+        rcopy(D.at[dp], D.at[dp], snd.at[7], rcv.at[3 if dy == 0 else 1], (q, sh)).start()
     arrived(240, 512, snd.at[0])
     arrived(192, 8192, snd.at[1])
     arrived(48, 8192, snd.at[2])
@@ -329,14 +339,20 @@
     arrived(64, 8192, snd.at[8])
     arrived(32, 8192, snd.at[9])
     lr_copy.wait()
-    arrived(112, 1024, rcv.at[3])
+    lr_own.wait()
+
+    def rows(h, b):
+        return jnp.concatenate([LR[h, cls, 2 * b:2 * b + 2].reshape(256, 128) for cls in range(2)], axis=1)
+
+    arrived(48, 1024, rcv.at[3])
+    near = D[pl.ds(yh * 4, 4)].reshape(256, 256)
+    for b in range(4):
+        U[b * 256:(b + 1) * 256, :] = jnp.dot(rows(yh, b), near, preferred_element_type=F32)
     arrived(112, 1024, snd.at[7])
-    d_own = D[pl.ds(c * 4, 4)].reshape(256, 256)
-    d_sib = D[pl.ds((1 - c) * 4, 4)].reshape(256, 256)
+    arrived(64, 1024, rcv.at[1])
+    far = D[pl.ds((1 - yh) * 4, 4)].reshape(256, 256)
     for b in range(4):
-        own = jnp.concatenate([W[h, yh, x, 2 * b:2 * b + 2].reshape(256, 128) for h in range(2)], axis=1)
-        oth = jnp.concatenate([LR[h, 2 * b:2 * b + 2].reshape(256, 128) for h in range(2)], axis=1)
-        u = jnp.dot(own, d_own, preferred_element_type=F32) + jnp.dot(oth, d_sib, preferred_element_type=F32)
+        u = U[b * 256:(b + 1) * 256, :] + jnp.dot(rows(1 - yh, b), far, preferred_element_type=F32)
         up_ref[b * 256:(b + 1) * 256, :] = u.astype(BF)
 
 
@@ -371,7 +387,8 @@
             pltpu.VMEM((64, 256), F32),
             pltpu.VMEM((2, 2, 32, 128), BF),
             pltpu.VMEM((2, 2, 4, 8, 2, 64, 128), BF),
-            pltpu.VMEM((2, 8, 2, 64, 128), BF),
+            pltpu.VMEM((2, 2, 8, 2, 64, 128), BF),
+            pltpu.VMEM((1024, 256), F32),
             pltpu.VMEM((512, 256), F32),
             pltpu.VMEM((2, 256, 512), BF),
             pltpu.VMEM((2, NCH, 2, 2, 4, 64, CW), BF),
@@ -385,7 +402,7 @@
             pltpu.VMEM((5, 2, 64, 128), F32),
             pltpu.VMEM((6, 2, 64, 128), F32),
             pltpu.VMEM((8, 64, 256), BF),
-            dma((5,)), dma((2,)), dma((2,)),
+            dma((6,)), dma((2,)), dma((2,)),
             dma((8,)), dma((2, 4)), dma((2, 4, 3)),
             dma((2,)), dma((4,)),
             dma((2, NCH, 2)), dma((NCH,)), dma((NCH,)),

time: 83.8 us -> 84.4 us (level)
  Pallas kernels: 82.6 us -> 83.7 us
    pallas_call x1, Pallas kernels: 81.8 us -> 82.8 us  [on_device(): pl.pallas_call(kernel, out_shape=(pltpu.VMEM((64, 256), F32), pltpu.VMEM(...]
where the time goes in v4:
time: 84.4 us; the launch traced here: 84.3 us
  Pallas kernels  83.7 us (99%)
    pallas_call x1, Pallas kernels, on_device(): pl.pallas_call(kernel, out_shape=(pltpu.VMEM((64, 256), F32), pltpu.VMEM(...  82.8 us

profile of v4, /device:TPU:32, one launch (start us, length us, event | category | flops | bytes accessed | tf_op | source)
XLA Modules:
  0.0 84.3 jit_solution(4599299235628311442)
XLA Ops:
  0.6 82.8 %galore.1 = (f32[64,256]{1,0:T(8,128)S(1)}, f32[64,256]{1,0:T(8,128)S(1)}, bf16[1024,256]{1,0:T(8,128)(2,1)S(1)}) custom-call(bf16[256,8192]{1,0:T(8,128)(2,1)} %tok_ref.1, bf16[256,8192]{1,0:T(8,128)(2,1)} %grad_ref.1, bf16[32,512]{1,0:T(8,128)(2,1)} %proj_ref.1, f32[64,256]{1,0:T(8,128)} %m1_ref.1, f32[64,256]{1,0:T(8,128)} %m2_ref.1), custom_call_target="tpu_custom_call" | custom-call | tf_op jit(solution)/shard_map/galore/pallas_call | solution.py:375
  83.5 0.9 %store_outputs.1 = (f32[64,256]{1,0:T(8,128)}, f32[64,256]{1,0:T(8,128)}, bf16[1024,256]{1,0:T(8,128)(2,1)}) custom-call(f32[64,256]{1,0:T(8,128)S(1)} %get-tuple-element.6.a_ref, f32[64,256]{1,0:T(8,128)S(1)} %get-tuple-element.7.b_ref, bf16[1024,256]{1,0:T(8,128)(2,1)S(1)} %get-tuple-element.8.u_ref), custom_call_target="tpu_custom_call" | custom-call | tf_op jit(solution)/shard_map/store_outputs/pallas_call | solution.py:416

commit v5 on v4

--- a/solution.py
+++ b/solution.py
@@ -159,10 +159,9 @@
         for cls in range(2):
             arrived(16, 4096, mr.at[cls, j])
             forward(cls, j)
-        for cls in range(2):
-            relay(cls, 0 if j == 1 else 1 if j == 3 else 3)
-    for cls in range(2):
-        relay(cls, 2)
+    for j in (0, 1, 3, 2):
+        for cls in range(2):
+            relay(cls, j)
     tok_own.wait()
     tok_ex.wait()
     ACC[...] = jnp.zeros_like(ACC)

time: 84.4 us -> 84 us (level)
  no operation moved by 1% of the time
where the time goes in v5:
time: 84 us; the launch traced here: 83.9 us
  Pallas kernels  83.2 us (99%)
    pallas_call x1, Pallas kernels, on_device(): pl.pallas_call(kernel, out_shape=(pltpu.VMEM((64, 256), F32), pltpu.VMEM(...  82.4 us

profile of v5, /device:TPU:32, one launch (start us, length us, event | category | flops | bytes accessed | tf_op | source)
XLA Modules:
  0.0 83.9 jit_solution(13956808839346731715)
XLA Ops:
  0.6 82.4 %galore.1 = (f32[64,256]{1,0:T(8,128)S(1)}, f32[64,256]{1,0:T(8,128)S(1)}, bf16[1024,256]{1,0:T(8,128)(2,1)S(1)}) custom-call(bf16[256,8192]{1,0:T(8,128)(2,1)} %tok_ref.1, bf16[256,8192]{1,0:T(8,128)(2,1)} %grad_ref.1, bf16[32,512]{1,0:T(8,128)(2,1)} %proj_ref.1, f32[64,256]{1,0:T(8,128)} %m1_ref.1, f32[64,256]{1,0:T(8,128)} %m2_ref.1), custom_call_target="tpu_custom_call" | custom-call | tf_op jit(solution)/shard_map/galore/pallas_call | solution.py:374
  83.0 0.9 %store_outputs.1 = (f32[64,256]{1,0:T(8,128)}, f32[64,256]{1,0:T(8,128)}, bf16[1024,256]{1,0:T(8,128)(2,1)}) custom-call(f32[64,256]{1,0:T(8,128)S(1)} %get-tuple-element.6.a_ref, f32[64,256]{1,0:T(8,128)S(1)} %get-tuple-element.7.b_ref, bf16[1024,256]{1,0:T(8,128)(2,1)S(1)} %get-tuple-element.8.u_ref), custom_call_target="tpu_custom_call" | custom-call | tf_op jit(solution)/shard_map/store_outputs/pallas_call | solution.py:415
